TPU v7x, 32 devices: a whole 2x2x4 slice. The times are simulated.
32 devices in a mesh: atoms: 8 (over z, core), loops: 4 (over y, x).
Axes of the slice: x: 2, y: 2, z: 4, core: 2. Of those that a mesh axis runs over, the one named last changes fastest.
Arguments:
- atom_site: int32 [32768], P('atoms'), may hold values from 0 to 65535, as said below
- loop_cells: int32 [3, 1024], P(None, 'loops'), may hold values from -200 to 199
- loop_burgers: int32 [1024], P('loops'), may hold values from 0 to 3
- loop_habit: int32 [1024], P('loops'), may hold values from 0 to 5
- loop_radius: float32 [1024], P('loops'), may hold values from 10 to 40
Outputs:
- log_intensity: float32 [64, 128, 128], P('loops', 'atoms')
Inputs may be any that keep to these rules, and one draw needn't show every extreme that they name: `atom_site`: site numbers are distinct; the first and the last site of the window are always occupied.
All inputs are finite; a program needn't handle non-finite values.
Results may differ from a plain program's by a relative error of at most 0.0003.
Values sent between devices are 32-bit elements; how exact they have to be, the bound alone decides.
A program may use at most 128 MiB of HBM per device.

v0:
```python
import math

import jax
import jax.numpy as jnp
import numpy as np
from jax import lax
from jax.sharding import PartitionSpec as P

WIN_X = 32
WIN_Y = 32
QX = 128
QY = 128
QZ = 64


LATTICE = 2.8665
POISSON = 0.29
TWO_PI = 2.0 * math.pi
BURGERS_TABLE = np.array(
    [[1.0, 1.0, 1.0], [-1.0, 1.0, 1.0], [1.0, -1.0, 1.0], [1.0, 1.0, -1.0]]
) * (0.5 * LATTICE)
NORMAL_TABLE = (
    np.array(
        [
            [1.0, 1.0, 0.0],
            [1.0, -1.0, 0.0],
            [1.0, 0.0, 1.0],
            [1.0, 0.0, -1.0],
            [0.0, 1.0, 1.0],
            [0.0, 1.0, -1.0],
        ]
    )
    * 0.70710678
)


def lookup(index, table):
    columns = []
    for column in range(3):
        total = jnp.zeros(index.shape, jnp.float32)
        for entry in range(table.shape[0]):
            total = total + jnp.where(
                index == entry, jnp.float32(table[entry, column]), jnp.float32(0.0)
            )
        columns.append(total)
    return jnp.stack(columns)


def site_anchor(site):
    basis = site % 2
    cell = site // 2
    first = cell % WIN_X
    second = cell // WIN_X % WIN_Y
    third = cell // (WIN_X * WIN_Y)
    cells = jnp.stack([first, second, third]).astype(jnp.float32)
    return LATTICE * (cells + 0.5 * basis.astype(jnp.float32)[None, :])


def loop_centre(cells):
    return LATTICE * (cells.astype(jnp.float32) + 0.25)


def loop_field(anchor, centre, burgers, normal, radius):
    offset = anchor[:, None, :] - centre[:, :, None]
    radius_sq = (radius * radius)[:, None]
    distance_sq = jnp.sum(offset * offset, axis=0) + radius_sq
    unit_dir = offset * lax.rsqrt(distance_sq)[None]
    along_b = jnp.sum(burgers[:, :, None] * unit_dir, axis=0)
    along_n = jnp.sum(normal[:, :, None] * unit_dir, axis=0)
    burgers_normal = jnp.sum(burgers * normal, axis=0)[:, None]
    strength = radius_sq / (8.0 * (1.0 - POISSON) * distance_sq)
    field = (1.0 - 2.0 * POISSON) * (
        burgers[:, :, None] * along_n[None] + normal[:, :, None] * along_b[None]
    )
    field = field - burgers_normal[None] * unit_dir + 3.0 * unit_dir * (along_b * along_n)[None]
    return jnp.sum(strength[None] * field, axis=1)


def waves(first, count, total, centre):
    steps = first + jnp.arange(count, dtype=jnp.float32)
    return TWO_PI / LATTICE * (centre + (steps - total * 0.5 + 0.5) / QX)


def factor_block(xcosines, xsines, zcosines, zsines, ytable):
    ywidth = ytable.shape[1] // 2
    left_real = (
        zcosines[None, :, :] * xcosines[:, None, :] - zsines[None, :, :] * xsines[:, None, :]
    )
    left_imag = (
        zcosines[None, :, :] * xsines[:, None, :] + zsines[None, :, :] * xcosines[:, None, :]
    )
    left_pair = jnp.stack([left_real, left_imag], axis=2)
    product = jnp.einsum(
        "xzca,ad->xzcd",
        left_pair,
        ytable,
        precision=lax.Precision.HIGHEST,
        preferred_element_type=jnp.float32,
    )
    real_part = product[:, :, 0, :ywidth] - product[:, :, 1, ywidth:]
    imag_part = product[:, :, 0, ywidth:] + product[:, :, 1, :ywidth]
    return jnp.stack([real_part, imag_part], axis=1)


def phase_tables(position, xwaves, ywaves, zwaves):
    xangle = xwaves[:, None] * position[0][None, :]
    yangle = position[1][:, None] * ywaves[None, :]
    zangle = zwaves[:, None] * position[2][None, :]
    ytable = jnp.concatenate([jnp.cos(yangle), jnp.sin(yangle)], axis=1)
    return (jnp.cos(xangle), jnp.sin(xangle), jnp.cos(zangle), jnp.sin(zangle), ytable)


def body(atom_site, loop_cells, loop_burgers, loop_habit, loop_radius):
    anchor = site_anchor(atom_site)
    centre = loop_centre(loop_cells)
    burgers = lookup(loop_burgers, BURGERS_TABLE)
    normal = lookup(loop_habit, NORMAL_TABLE)
    loop_count = centre.shape[1]
    block_size = math.gcd(loop_count, 64)

    def add_block(number, running):
        begin = number * block_size
        return running + loop_field(
            anchor,
            lax.dynamic_slice_in_dim(centre, begin, block_size, 1),
            lax.dynamic_slice_in_dim(burgers, begin, block_size, 1),
            lax.dynamic_slice_in_dim(normal, begin, block_size, 1),
            lax.dynamic_slice_in_dim(loop_radius, begin, block_size, 0),
        )

    partial_field = lax.fori_loop(
        0, loop_count // block_size, add_block, jnp.zeros(anchor.shape, jnp.float32)
    )
    displacement = lax.psum(partial_field, "loops")
    position = anchor + displacement
    group_count = lax.axis_size("atoms")
    zrows = QZ // lax.axis_size("loops")
    atom_total = position.shape[1] * group_count
    zfirst = (lax.axis_index("loops") * zrows).astype(jnp.float32)
    zwaves = waves(zfirst, zrows, QZ, 0.0)
    ywaves = waves(jnp.float32(0.0), QY, QY, 1.0)
    xwaves = waves(jnp.float32(0.0), QX, QX, 1.0)
    xcosines, xsines, zcosines, zsines, ytable = phase_tables(position, xwaves, ywaves, zwaves)
    summed = lax.psum_scatter(
        factor_block(xcosines, xsines, zcosines, zsines, ytable),
        "atoms",
        scatter_dimension=0,
        tiled=True,
    )
    power = summed[:, 0] ** 2 + summed[:, 1] ** 2
    return jnp.log1p(jnp.transpose(power, (1, 0, 2)) / atom_total)


def solution(mesh):
    placed = (P("atoms"), P(None, "loops"), P("loops"), P("loops"), P("loops"))
    return jax.shard_map(
        body, mesh=mesh, in_specs=placed, out_specs=P("loops", "atoms", None), check_vma=False
    )
```

profile of v0, /device:TPU:0, one launch (start us, length us, event | category | flops | bytes accessed | tf_op | source)
XLA Modules:
  0.0 187.0 jit_solution(17703038132676561557)
XLA Ops:
  6.5 0.8 add_select_fusion.4
  7.3 0.7 fusion.29
  8.1 0.7 select_add_fusion.2
  8.8 0.7 select_add_fusion.7
  9.4 0.7 add_multiply_fusion
  10.2 17.1 %while.14 = (s32[]{:T(128)}, f32[3,4096]{1,0:T(4,128)S(1)}, f32[256]{0:T(256)}, f32[3,4096]{1,0:T(4,128)S(1)}, f32[3,256]{1,0:T(4,128)S(1)}, /*index=5*/f32[3,25...) while((s32[]{:T(128)}, f32[3,4096]{1,0:T(4,128)S(1)}, ...), condition=%wide.region_6.7_spmd.clone, body=%wide.region_0.6_spmd.clone.sunk | while | flops 17052036 | bytes 16084141 | solution.py:131
  10.2 0.1 multiply_reduce_fusion.2
  10.3 0.4 fusion.44
  10.7 0.8 dynamic-slice_multiply_fusion.2
  11.5 0.3 multiply_divide_fusion.2
  11.8 0.9 fusion.45
  12.7 0.1 multiply_multiply_fusion.2
  12.8 1.6 fusion.46
  14.4 0.1 select_add_fusion.10
  14.5 0.1 multiply_reduce_fusion.2
  14.6 0.4 fusion.44
  15.0 0.8 dynamic-slice_multiply_fusion.2
  15.8 0.3 multiply_divide_fusion.2
  16.1 0.9 fusion.45
  17.0 0.1 multiply_multiply_fusion.2
  17.1 1.6 fusion.46
  18.7 0.1 select_add_fusion.10
  18.8 0.1 multiply_reduce_fusion.2
  18.9 0.4 fusion.44
  19.3 0.8 dynamic-slice_multiply_fusion.2
  20.0 0.3 multiply_divide_fusion.2
  20.4 0.9 fusion.45
  21.3 0.1 multiply_multiply_fusion.2
  21.4 1.6 fusion.46
  23.0 0.1 select_add_fusion.10
  23.0 0.1 multiply_reduce_fusion.2
  23.1 0.4 fusion.44
  23.5 0.8 dynamic-slice_multiply_fusion.2
  24.3 0.3 multiply_divide_fusion.2
  24.7 0.9 fusion.45
  25.5 0.1 multiply_multiply_fusion.2
  25.6 1.6 fusion.46
  27.3 18.6 %psum.7 = f32[3,4096]{1,0:T(4,128)S(1)} all-reduce(f32[3,4096]{1,0:T(4,128)S(1)} %get-tuple-element.129), channel_id=1, replica_groups=mesh['atoms'=8,'loops'=4] {'loops'}, use_global_device_ids=true, to_apply=%region_7.8 | all-reduce | flops 12288 | bytes 98304 | tf_op jit(solution)/shard_map/psum | solution.py:134
  46.0 7.3 %multiply_cosine_fusion.1 = (f32[128,4096]{1,0:T(8,128)S(1)}, f32[128,4096]{1,0:T(8,128)S(1)}) fusion(f32[4096]{0:T(1024)S(1)} %bitcast.45, f32[128]{0:T(128)S(1)} %add_multiply_fusion.1), kind=kLoop, calls=%fused_computation.34 | loop fusion | flops 524288 | bytes 4211200 | tf_op jit(solution)/shard_map/cos | solution.py:110
  53.3 7.5 %multiply_cosine_fusion = (f32[4096,128]{1,0:T(8,128)S(1)}, f32[4096,128]{1,0:T(8,128)S(1)}) fusion(f32[128]{0:T(128)S(1)} %add_multiply_fusion.1, f32[4096]{0:T(1024)S(1)} %bitcast.44), kind=kLoop, calls=%fused_computation.32 | loop fusion | flops 524288 | bytes 4211200 | tf_op jit(solution)/shard_map/cos | solution.py:109
  60.8 1.0 multiply_cosine_fusion.2
  61.8 22.0 %multiply_subtract_fusion = (f32[128,16,1,4096]{3,0,2,1:T(8,128)}, f32[128,16,1,4096]{3,0,2,1:T(8,128)}) fusion(f32[128,4096]{1,0:T(8,128)S(1)} %get-tuple-element.186, f32[16,4096]{1,0:T(8,128)S(1)} %get-tuple-element.184, f32[128,4096]{1,0:T(8,128)S(1)} %get-tuple-element.185, f32[16,4096]{1,0:T(8,128)S(1)} %get-tuple-element.183), kind=kLoop, calls=%fused_computation.27 | loop fusion | flops 50331648 | bytes 71827456 | tf_op jit(solution)/shard_map/sub | solution.py:87
  83.8 57.6 %fusion.11 = f32[128,16,2,256]{3,0,2,1:T(8,128)S(1)} fusion(f32[128,16,1,4096]{3,0,2,1:T(8,128)} %get-tuple-element.177, f32[128,16,1,4096]{3,0,2,1:T(8,128)} %get-tuple-element.176, f32[4096,128]{1,0:T(8,128)S(1)} %get-tuple-element.182, f32[4096,128]{1,0:T(8,128)S(1)} %get-tuple-element.181), kind=kOutput, calls=%fused_computation.22 | convolution fusion | flops 51557433344 | bytes 75497472 | tf_op jit(solution)/shard_map/xzca,ad->xzcd/dot_general | solution.py:93
  141.3 0.1 fusion.17
  141.5 0.1 fusion.19
  141.6 1.5 pad_maximum_fusion
  143.1 35.4 %reduce-scatter.2.cloned.1.call-done = f32[16,2,16,128]{3,0,2,1:T(8,128)} async-done(((f32[128,2,16,128]{3,0,2,1:T(8,128)}), f32[16,2,16,128]{3,0,2,1:T(8,128)}) %reduce-scatter.2.cloned.1.call-update) | async-done | bytes 262160 | tf_op jit(solution)/shard_map/reduce_scatter | solution.py:144
  178.5 1.7 fusion.23
  (10 shorter events, 0.3 us)
Async XLA Ops:
  6.5 171.9 %reduce-scatter.2.cloned.1.call-start = ((), (), s32[]{:S(2)}) async-start(), calls=%async_computation.1 | async-start | bytes 2359296 | tf_op jit(solution)/shard_map/reduce_scatter | solution.py:144
Sparse Core Ops, SparseCore 0:
  143.2 35.2 reduce-scatter.1
where the time goes:
time: 187 us
  other arithmetic  61.8 us (33%)
  matrix products  57.6 us (31%)
  waiting for transfers between devices  35.4 us (19%)
  blocking collectives  18.6 us (10%)
  between operations  13.5 us (7%)
    dot_general x1, matrix products, factor_block(): jnp.einsum('xzca,ad->xzcd', left_pair, ytable, precision=lax.Precision.HI...  57.6 us
    reduce_scatter x1, waiting for transfers between devices, body(): lax.psum_scatter(factor_block(xcosines, xsines, zcosines, zsines, ytable)...  35.4 us
    sub x1, other arithmetic, factor_block(): zcosines[None, :, :] * xcosines[:, None, :]  22 us
    psum x1, blocking collectives, body(): displacement = lax.psum(partial_field, 'loops')  18.6 us
    cos x1, other arithmetic, phase_tables(): ytable = jnp.concatenate([jnp.cos(yangle), jnp.sin(yangle)], axis=1)  7.51 us
    cos x1, other arithmetic, phase_tables(): jnp.cos(xangle)  7.29 us
    reduce_sum x4, other arithmetic, loop_field(): return jnp.sum(strength[None] * field, axis=1)  6.33 us
  transfers between devices with their start and end apart: 1, of which 1 were waited for; matrix products, arithmetic and copies ran while one was open for 0% of the time, Pallas kernels for 0%

commit v1 on v0

v1 whole, which is shorter than its diff:
```python
import functools
import math

import jax
import jax.numpy as jnp
import numpy as np
from jax import lax
from jax.experimental import pallas as pl
from jax.experimental.pallas import tpu as pltpu
from jax.sharding import PartitionSpec as P

WIN_X = 32
WIN_Y = 32
QX = 128
QY = 128
QZ = 64
LANES = 128

LATTICE = 2.8665
POISSON = 0.29
MIX = 1.0 - 2.0 * POISSON
BURGERS_TABLE = np.array(
    [[1.0, 1.0, 1.0], [-1.0, 1.0, 1.0], [1.0, -1.0, 1.0], [1.0, 1.0, -1.0]]
) * (0.5 * LATTICE)
NORMAL_TABLE = (
    np.array(
        [
            [1.0, 1.0, 0.0],
            [1.0, -1.0, 0.0],
            [1.0, 0.0, 1.0],
            [1.0, 0.0, -1.0],
            [0.0, 1.0, 1.0],
            [0.0, 1.0, -1.0],
        ]
    )
    * 0.70710678
)


def fit(function, degree):
    nodes = 0.125 * (1.0 + np.cos(np.pi * (np.arange(64) + 0.5) / 64))
    series = np.polynomial.Chebyshev.fit(nodes, function(np.sqrt(nodes)), degree, domain=[0.0, 0.25])
    return [float(c) for c in series.convert(kind=np.polynomial.Polynomial).coef]


COSINE = fit(lambda r: np.cos(2.0 * np.pi * r), 6)
SINE = fit(lambda r: np.sin(2.0 * np.pi * r) / r, 6)


def horner(coefs, u):
    total = jnp.float32(coefs[-1])
    for c in reversed(coefs[:-1]):
        total = total * u + jnp.float32(c)
    return total


def cos_turns(t):
    r = t - jnp.round(t)
    return horner(COSINE, r * r)


def cos_sin_turns(t):
    r = t - jnp.round(t)
    u = r * r
    return horner(COSINE, u), r * horner(SINE, u)


def lookup(index, table, column):
    total = jnp.zeros(index.shape, jnp.float32)
    for entry in range(table.shape[0]):
        total = jnp.where(index == entry, jnp.float32(table[entry, column]), total)
    return total


def field_kernel(
    group_count, site_ref, cells_ref, burgers_ref, habit_ref, radius_ref, out_ref, params_ref, anchor_ref
):
    loops = cells_ref.shape[1]
    chunks = site_ref.shape[0]
    burgers = [lookup(burgers_ref[...], BURGERS_TABLE, c) for c in range(3)]
    normal = [lookup(habit_ref[...], NORMAL_TABLE, c) for c in range(3)]
    centre = [LATTICE * (cells_ref[c : c + 1, :].astype(jnp.float32) + 0.25) for c in range(3)]
    radius_sq = radius_ref[...] * radius_ref[...]
    overlap = burgers[0] * normal[0] + burgers[1] * normal[1] + burgers[2] * normal[2]
    ratio = 3.0 / MIX
    rows = (
        centre
        + [radius_sq]
        + burgers
        + [ratio * n for n in normal]
        + [(1.0 / ratio) * b for b in burgers]
        + normal
        + [(MIX / (8.0 * (1.0 - POISSON))) * radius_sq, (1.0 / MIX) * overlap]
    )
    count = len(rows)
    rows = rows + [jnp.zeros((1, loops), jnp.float32)] * (-count % 8)
    columns = jnp.concatenate(rows, axis=0).T
    for number in range(count):
        params_ref[number] = jnp.broadcast_to(columns[:, number : number + 1], (loops, LANES))

    site = site_ref[...]
    basis = 0.5 * (site & 1).astype(jnp.float32)
    cell = lax.shift_right_logical(site, 1)
    first = lax.rem(cell, WIN_X)
    second = lax.rem(lax.div(cell, WIN_X), WIN_Y)
    third = lax.div(cell, WIN_X * WIN_Y)
    for axis, index in enumerate((first, second, third)):
        anchor_ref[axis] = LATTICE * (index.astype(jnp.float32) + basis)

    width = 2

    def chunk_step(step, _):
        anchors = [
            [
                jnp.broadcast_to(anchor_ref[axis, pl.ds(step * width + w, 1), :], (8, LANES))
                for axis in range(3)
            ]
            for w in range(width)
        ]

        def loop_step(group, sums):
            at = pl.ds(pl.multiple_of(group * 8, 8), 8)
            p = [params_ref[number, at, :] for number in range(count)]
            new = []
            for w in range(width):
                d = [anchors[w][c] - p[c] for c in range(3)]
                s = d[0] * d[0] + d[1] * d[1] + d[2] * d[2] + p[3]
                root = lax.rsqrt(s)
                inv = root * root
                scale = inv * root * p[16]
                along_b = p[4] * d[0] + p[5] * d[1] + p[6] * d[2]
                along_n = p[7] * d[0] + p[8] * d[1] + p[9] * d[2]
                weight_b = scale * along_n
                weight_n = scale * along_b
                weight_d = scale * (along_b * along_n * inv - p[17])
                for c in range(3):
                    new.append(
                        sums[3 * w + c] + (p[10 + c] * weight_b + p[13 + c] * weight_n + d[c] * weight_d)
                    )
            return tuple(new)

        zero = jnp.zeros((8, LANES), jnp.float32)
        sums = lax.fori_loop(0, loops // 8, loop_step, (zero,) * (3 * width), unroll=2)
        for w in range(width):
            for c in range(3):
                total = jnp.sum(sums[3 * w + c], axis=0, keepdims=True)
                out_ref[c, pl.ds(step * width + w, 1), :] = (
                    total + (1.0 / group_count) * anchor_ref[c, pl.ds(step * width + w, 1), :]
                )
        return 0

    lax.fori_loop(0, chunks // width, chunk_step, 0)


def exchange_kernel(na, nl, part_ref, out_ref, landed, send_a, recv_a, send_b, recv_b, send_c, recv_c):
    me_a = lax.axis_index("atoms")
    me_l = lax.axis_index("loops")
    mesh_ids = pl.DeviceIdType.MESH
    peers_a = [lax.rem(me_a + o, na) for o in range(1, na)]
    peers_l = [lax.rem(me_l + o, nl) for o in range(1, nl)]
    barrier = pltpu.get_barrier_semaphore()
    for peer in peers_a:
        pl.semaphore_signal(barrier, inc=1, device_id=(peer, me_l), device_id_type=mesh_ids)
    for peer in peers_l:
        pl.semaphore_signal(barrier, inc=1, device_id=(me_a, peer), device_id_type=mesh_ids)
    pl.semaphore_wait(barrier, na + nl - 2)

    def send(src, dst, send_sem, recv_sem, peer):
        copy = pltpu.make_async_remote_copy(
            src_ref=src,
            dst_ref=dst,
            send_sem=send_sem,
            recv_sem=recv_sem,
            device_id=peer,
            device_id_type=mesh_ids,
        )
        copy.start()
        return copy

    first = [
        send(part_ref.at[peer], landed.at[o], send_a.at[o], recv_a.at[o], (me_a, peer))
        for o, peer in enumerate(peers_l)
    ]
    total = part_ref[me_l]
    for o, copy in enumerate(first):
        copy.wait_recv()
        total = total + landed[o]
    out_ref[0, 0] = total
    second = [
        send(out_ref.at[0, 0], out_ref.at[0, o + 1], send_b.at[o], recv_b.at[o], (peer, me_l))
        for o, peer in enumerate(peers_a)
    ]
    for copy in second:
        copy.wait_recv()
    third = [
        send(out_ref.at[0], out_ref.at[o + 1], send_c.at[o], recv_c.at[o], (me_a, peer))
        for o, peer in enumerate(peers_l)
    ]
    for copy in third:
        copy.wait_recv()
    for copy in first + second + third:
        copy.wait_send()


def split(value):
    high = value.astype(jnp.bfloat16)
    low = (value - high.astype(jnp.float32)).astype(jnp.bfloat16)
    return high, low


def amplitude_kernel(atom_total, zrows, xrows, pos_ref, out_ref, acc_ref):
    slots, _, rows, _ = pos_ref.shape
    zhalf, xhalf, yhalf = zrows // 2, xrows // 2, QY // 2
    inverse = 1.0 / LATTICE
    step = inverse / QX
    xmid = 1.0 + (lax.axis_index("atoms") * xrows + xhalf - QX // 2).astype(jnp.float32) / QX
    zmid = (lax.axis_index("loops") * zrows + zhalf - QZ // 2).astype(jnp.float32) / QX
    wide = LANES

    def sub_iota(count):
        return lax.broadcasted_iota(jnp.int32, (count, wide), 0)

    def half_factors(half):
        number = sub_iota(2 * half)
        is_sine = number >= half
        index = jnp.where(is_sine, number - half, number).astype(jnp.float32)
        return (index + 0.5) * step, jnp.where(is_sine, 0.25, 0.0).astype(jnp.float32)

    zfactor, zshift = half_factors(zhalf)
    xfactor, xshift = half_factors(xhalf)
    fine = (sub_iota(8).astype(jnp.float32) - 3.5) * step
    blocks = yhalf // 16
    coarse_number = sub_iota(8)
    coarse = jnp.where(
        coarse_number < blocks, 4.0 + 8.0 * coarse_number.astype(jnp.float32), 0.5 * yhalf
    ) * step

    def tables(x, y, z):
        ztab = cos_turns(z * zfactor - zshift)
        xtab = cos_turns(x * xfactor - xshift)
        base = (x * xmid + z * zmid + y) * inverse
        base = base - jnp.round(base)
        dr, di = cos_sin_turns(base + y * fine)
        cc, cs = cos_sin_turns(y * coarse)
        left = jnp.concatenate([xtab[n : n + 1, :] * ztab for n in range(2 * xhalf)], axis=0)
        real = [None] * (2 * blocks)
        imag = [None] * (2 * blocks)
        for k in range(blocks):
            c, s = cc[k : k + 1, :], cs[k : k + 1, :]
            rc, rs, ic, is_ = dr * c, dr * s, di * c, di * s
            real[blocks + k], imag[blocks + k] = rc - is_, ic + rs
            real[blocks - 1 - k], imag[blocks - 1 - k] = rc + is_, ic - rs
        turned = jnp.concatenate(real + imag, axis=0)
        right = jnp.concatenate(
            [turned * cc[blocks : blocks + 1, :], turned * cs[blocks : blocks + 1, :]], axis=0
        )
        return split(left) + split(right)

    contract = (((1,), (1,)), ((), ()))

    def dot(a, b):
        return lax.dot_general(a, b, contract, preferred_element_type=jnp.float32)

    acc_ref[...] = jnp.zeros_like(acc_ref)
    mrows = left_rows = 4 * zhalf * xhalf
    pair = min(2, rows)

    def slot_step(slot, _):
        total = None
        for row in range(0, rows, pair):
            parts = []
            for r in range(row, row + pair):
                x, y, z = (pos_ref[slot, c, r : r + 1, :] for c in range(3))
                parts.append(tables(x, y, z))
            lh, ll, rh, rl = (jnp.concatenate([p[n] for p in parts], axis=1) for n in range(4))
            both = dot(jnp.concatenate([lh, ll], axis=0), rh)
            here = both[:mrows] + both[mrows:] + dot(lh, rl)
            total = here if total is None else total + here
        acc_ref[...] += total
        return 0

    lax.fori_loop(0, slots, slot_step, 0)

    acc = acc_ref[...]
    cre, cim = acc[:, :yhalf], acc[:, yhalf : 2 * yhalf]
    sre, sim = acc[:, 2 * yhalf : 3 * yhalf], acc[:, 3 * yhalf :]
    re = jnp.concatenate([cre + sim, cre - sim], axis=1)
    im = jnp.concatenate([cim - sre, cim + sre], axis=1)

    def rows_of(value, xt, mx, zt):
        begin = ((xt * xhalf + mx) * 2 + zt) * zhalf
        return value[begin : begin + zhalf]

    for mx in range(xhalf):
        by_z = {}
        for xt in range(2):
            rc, rs = rows_of(re, xt, mx, 0), rows_of(re, xt, mx, 1)
            ic, is_ = rows_of(im, xt, mx, 0), rows_of(im, xt, mx, 1)
            by_z[xt, 1] = (rc - is_, ic + rs)
            by_z[xt, 0] = (rc + is_, ic - rs)
        for zsign in range(2):
            (rc, ic), (rs, is_) = by_z[0, zsign], by_z[1, zsign]
            for xsign, power in (
                (1, (rc - is_) ** 2 + (ic + rs) ** 2),
                (0, (rc + is_) ** 2 + (ic - rs) ** 2),
            ):
                value = jnp.log1p(power / atom_total)
                xi = xhalf + mx if xsign else xhalf - 1 - mx
                for mz in range(zhalf):
                    zi = zhalf + mz if zsign else zhalf - 1 - mz
                    out_ref[zi, xi : xi + 1, :] = value[mz : mz + 1, :]


def body(na, nl, atom_site, loop_cells, loop_burgers, loop_habit, loop_radius):
    atoms = atom_site.shape[0]
    loops = loop_cells.shape[1]
    chunks = atoms // LANES
    rows = chunks // nl
    vmem = pl.BlockSpec(memory_space=pltpu.VMEM)
    partial_field = pl.pallas_call(
        functools.partial(field_kernel, nl),
        out_shape=jax.ShapeDtypeStruct((3, chunks, LANES), jnp.float32),
        in_specs=[vmem] * 5,
        out_specs=vmem,
        scratch_shapes=[
            pltpu.VMEM((18, loops, LANES), jnp.float32),
            pltpu.VMEM((3, chunks, LANES), jnp.float32),
        ],
        compiler_params=pltpu.CompilerParams(vmem_limit_bytes=32 * 2**20),
        name="loop_field",
    )(
        atom_site.reshape(chunks, LANES),
        loop_cells,
        loop_burgers.reshape(1, loops),
        loop_habit.reshape(1, loops),
        loop_radius.reshape(1, loops),
    )
    pieces = jnp.transpose(partial_field.reshape(3, nl, rows, LANES), (1, 0, 2, 3))
    position = pl.pallas_call(
        functools.partial(exchange_kernel, na, nl),
        out_shape=jax.ShapeDtypeStruct((nl, na, 3, rows, LANES), jnp.float32),
        in_specs=[vmem],
        out_specs=vmem,
        scratch_shapes=[pltpu.VMEM((nl - 1, 3, rows, LANES), jnp.float32)]
        + [pltpu.SemaphoreType.DMA((n - 1,)) for n in (nl, nl, na, na, nl, nl)],
        compiler_params=pltpu.CompilerParams(
            collective_id=0, has_side_effects=True, vmem_limit_bytes=32 * 2**20
        ),
        name="exchange_positions",
    )(pieces)
    zrows, xrows = QZ // nl, QX // na
    return pl.pallas_call(
        functools.partial(amplitude_kernel, float(atoms * na), zrows, xrows),
        out_shape=jax.ShapeDtypeStruct((zrows, xrows, QY), jnp.float32),
        in_specs=[vmem],
        out_specs=vmem,
        scratch_shapes=[pltpu.VMEM((zrows * xrows, 2 * QY), jnp.float32)],
        compiler_params=pltpu.CompilerParams(vmem_limit_bytes=48 * 2**20),
        name="amplitude",
    )(position.reshape(nl * na, 3, rows, LANES))


def solution(mesh):
    placed = (P("atoms"), P(None, "loops"), P("loops"), P("loops"), P("loops"))
    return jax.shard_map(
        functools.partial(body, mesh.shape["atoms"], mesh.shape["loops"]),
        mesh=mesh,
        in_specs=placed,
        out_specs=P("loops", "atoms", None),
        check_vma=False,
    )
```

time: 187 us -> 57 us (0.30)
  other arithmetic: 61.8 us -> 0 us
  matrix products: 57.6 us -> 0 us
  Pallas kernels: 0 us -> 55.2 us
  waiting for transfers between devices: 35.4 us -> 0 us
  blocking collectives: 18.6 us -> 0 us
  between operations: 13.5 us -> 0.03 us
    dot_general x1 -> x0, matrix products: 57.6 us -> none  [factor_block(): jnp.einsum('xzca,ad->xzcd', left_pair, ytable, precision=lax.Precision.HI...]
    pallas_call x0 -> x3, Pallas kernels: none -> 55.2 us  [the longest x1 27.3 us: body(): pl.pallas_call(functools.partial(amplitude_kernel, float(atoms * na), zro...]
    reduce_scatter x1 -> x0, waiting for transfers between devices: 35.4 us -> none  [body(): lax.psum_scatter(factor_block(xcosines, xsines, zcosines, zsines, ytable)...]
    sub x2 -> x0, other arithmetic: 22.1 us -> none  [the longest x1 22 us: factor_block(): zcosines[None, :, :] * xcosines[:, None, :]]
    psum x1 -> x0, blocking collectives: 18.6 us -> none  [body(): displacement = lax.psum(partial_field, 'loops')]
    cos x3 -> x0, other arithmetic: 15.8 us -> none  [the longest x1 7.51 us: phase_tables(): ytable = jnp.concatenate([jnp.cos(yangle), jnp.sin(yangle)], axis=1)]
    reduce_sum x16 -> x0, other arithmetic: 11.7 us -> none  [the longest x4 6.33 us: loop_field(): return jnp.sum(strength[None] * field, axis=1)]
    mul x13 -> x0, other arithmetic: 4.97 us -> none  [the longest x4 3.04 us: loop_field(): radius_sq = (radius * radius)[:, None]]
  transfers between devices with their start and end apart: 1 -> 0, of which waited for: 1 -> 0; matrix products, arithmetic and copies ran while one was open for 0% -> 0% of each run, Pallas kernels for 0% -> 0%
where the time goes in v1:
time: 57 us; the launch traced here: 56.7 us
  Pallas kernels  55.2 us (97%)
  local copies, waits for them, and re-layouts  1.44 us (3%)
    pallas_call x1, Pallas kernels, body(): pl.pallas_call(functools.partial(amplitude_kernel, float(atoms * na), zro...  27.3 us
    pallas_call x1, Pallas kernels, body(): pl.pallas_call(functools.partial(exchange_kernel, na, nl), out_shape=jax....  18.6 us
    pallas_call x1, Pallas kernels, body(): pl.pallas_call(functools.partial(field_kernel, nl), out_shape=jax.ShapeDt...  9.3 us
    unnamed x10, local copies, waits for them, and re-layouts  1.44 us

profile of v1, /device:TPU:0, one launch (start us, length us, event | category | flops | bytes accessed | tf_op | source)
XLA Modules:
  0.0 56.7 jit_solution(6896365682182737296)
XLA Ops:
  0.0 0.0 copy-start.1
  0.0 0.0 copy-start.3
  0.0 0.0 copy-start.4
  0.0 0.0 copy-start.2
  0.0 0.7 %copy-done.1 = s32[3,256]{1,0:T(4,128)S(1)} copy-done((s32[3,256]{1,0:T(4,128)S(1)}, s32[3,256]{1,0:T(4,128)}, u32[]{:S(2)}) %copy-start.1) | copy-done | bytes 3096
  0.7 0.0 copy-done.3
  0.7 0.0 copy-done.4
  0.7 0.0 copy-done.2
  0.7 0.0 copy-start
  0.7 0.7 %copy-done = s32[4096]{0:T(1024)S(1)} copy-done((s32[4096]{0:T(1024)S(1)}, s32[4096]{0:T(1024)}, u32[]{:S(2)}) %copy-start) | copy-done | bytes 16408
  1.4 9.3 %loop_field.1 = f32[3,32,128]{2,1,0:T(8,128)S(1)} custom-call(s32[32,128]{1,0:T(8,128)S(1)} %bitcast.11, s32[3,256]{1,0:T(4,128)S(1)} %copy-done.1, s32[1,256]{1,0:T(1,128)S(1)} %bitcast.12, s32[1,256]{1,0:T(1,128)S(1)} %bitcast.13, f32[1,256]{1,0:T(1,128)S(1)} %bitcast.14), custom_call_target="tpu_custom_call" | custom-call | tf_op jit(solution)/shard_map/loop_field/pallas_call | solution.py:320
  10.8 18.6 %exchange_positions.1 = f32[4,8,3,8,128]{4,3,2,1,0:T(8,128)S(1)} custom-call(f32[4,3,8,128]{3,2,1,0:T(8,128)S(1)} %copy_bitcast_fusion.part_ref), custom_call_target="tpu_custom_call" | custom-call | tf_op jit(solution)/shard_map/exchange_positions/pallas_call | solution.py:339
  29.4 27.3 %amplitude.1 = f32[16,16,128]{2,1,0:T(8,128)} custom-call(f32[32,3,8,128]{3,2,1,0:T(8,128)S(1)} %bitcast.10), custom_call_target="tpu_custom_call" | custom-call | tf_op jit(solution)/shard_map/amplitude/pallas_call | solution.py:352
  (1 shorter events, 0.0 us)
Async XLA Ops:
  0.0 0.7 %copy-start.1 = (s32[3,256]{1,0:T(4,128)S(1)}, s32[3,256]{1,0:T(4,128)}, u32[]{:S(2)}) copy-start(s32[3,256]{1,0:T(4,128)} %cells_ref.1) | copy-start | bytes 9220
  0.0 0.7 %copy-start.3 = (s32[256]{0:T(256)S(1)}, s32[256]{0:T(256)}, u32[]{:S(2)}) copy-start(s32[256]{0:T(256)} %param.8) | copy-start | bytes 3076
  0.0 0.7 %copy-start.4 = (f32[256]{0:T(256)S(1)}, f32[256]{0:T(256)}, u32[]{:S(2)}) copy-start(f32[256]{0:T(256)} %param.9) | copy-start | bytes 3076
  0.0 0.7 %copy-start.2 = (s32[256]{0:T(256)S(1)}, s32[256]{0:T(256)}, u32[]{:S(2)}) copy-start(s32[256]{0:T(256)} %param.7) | copy-start | bytes 3076
  0.7 0.7 %copy-start = (s32[4096]{0:T(1024)S(1)}, s32[4096]{0:T(1024)}, u32[]{:S(2)}) copy-start(s32[4096]{0:T(1024)} %param.5) | copy-start | bytes 49156

commit v2 on v1

v2 whole, which is shorter than its diff:
```python
import functools
import math

import jax
import jax.numpy as jnp
import numpy as np
from jax import lax
from jax.experimental import pallas as pl
from jax.experimental.pallas import tpu as pltpu
from jax.sharding import PartitionSpec as P

WIN_X = 32
WIN_Y = 32
QX = 128
QY = 128
QZ = 64
LANES = 128

LATTICE = 2.8665
POISSON = 0.29
MIX = 1.0 - 2.0 * POISSON
BURGERS_TABLE = np.array(
    [[1.0, 1.0, 1.0], [-1.0, 1.0, 1.0], [1.0, -1.0, 1.0], [1.0, 1.0, -1.0]]
) * (0.5 * LATTICE)
NORMAL_TABLE = (
    np.array(
        [
            [1.0, 1.0, 0.0],
            [1.0, -1.0, 0.0],
            [1.0, 0.0, 1.0],
            [1.0, 0.0, -1.0],
            [0.0, 1.0, 1.0],
            [0.0, 1.0, -1.0],
        ]
    )
    * 0.70710678
)


def fit(function, degree):
    nodes = 0.125 * (1.0 + np.cos(np.pi * (np.arange(64) + 0.5) / 64))
    series = np.polynomial.Chebyshev.fit(nodes, function(np.sqrt(nodes)), degree, domain=[0.0, 0.25])
    return [float(c) for c in series.convert(kind=np.polynomial.Polynomial).coef]


COSINE = fit(lambda r: np.cos(2.0 * np.pi * r), 6)
SINE = fit(lambda r: np.sin(2.0 * np.pi * r) / r, 6)


def horner(coefs, u):
    total = jnp.float32(coefs[-1])
    for c in reversed(coefs[:-1]):
        total = total * u + jnp.float32(c)
    return total


def cos_turns(t):
    r = t - jnp.round(t)
    return horner(COSINE, r * r)


def cos_sin_turns(t):
    r = t - jnp.round(t)
    u = r * r
    return horner(COSINE, u), r * horner(SINE, u)


def lookup(index, table, column):
    total = jnp.zeros(index.shape, jnp.float32)
    for entry in range(table.shape[0]):
        total = jnp.where(index == entry, jnp.float32(table[entry, column]), total)
    return total


def field_phase(
    nl, site_ref, cells_ref, burgers_ref, habit_ref, radius_ref, part_ref, params_ref, anchor_ref
):
    loops = cells_ref.shape[1]
    chunks = site_ref.shape[0]
    rows_each = part_ref.shape[2]
    burgers = [lookup(burgers_ref[...], BURGERS_TABLE, c) for c in range(3)]
    normal = [lookup(habit_ref[...], NORMAL_TABLE, c) for c in range(3)]
    centre = [LATTICE * (cells_ref[c : c + 1, :].astype(jnp.float32) + 0.25) for c in range(3)]
    radius_sq = radius_ref[...] * radius_ref[...]
    overlap = burgers[0] * normal[0] + burgers[1] * normal[1] + burgers[2] * normal[2]
    ratio = 3.0 / MIX
    rows = (
        centre
        + [radius_sq]
        + burgers
        + [ratio * n for n in normal]
        + [(1.0 / ratio) * b for b in burgers]
        + normal
        + [(MIX / (8.0 * (1.0 - POISSON))) * radius_sq, (1.0 / MIX) * overlap]
    )
    count = len(rows)
    rows = rows + [jnp.zeros((1, loops), jnp.float32)] * (-count % 8)
    columns = jnp.concatenate(rows, axis=0).T
    for number in range(count):
        params_ref[number] = jnp.broadcast_to(columns[:, number : number + 1], (loops, LANES))

    site = site_ref[...]
    basis = 0.5 * (site & 1).astype(jnp.float32)
    cell = lax.shift_right_logical(site, 1)
    first = lax.rem(cell, WIN_X)
    second = lax.rem(lax.div(cell, WIN_X), WIN_Y)
    third = lax.div(cell, WIN_X * WIN_Y)
    for axis, index in enumerate((first, second, third)):
        anchor_ref[axis] = LATTICE * (index.astype(jnp.float32) + basis)

    width = 4

    def chunk_step(step, _):
        anchors = [
            [
                jnp.broadcast_to(anchor_ref[axis, pl.ds(step * width + w, 1), :], (8, LANES))
                for axis in range(3)
            ]
            for w in range(width)
        ]

        def loop_step(group, sums):
            at = pl.ds(pl.multiple_of(group * 8, 8), 8)
            p = [params_ref[number, at, :] for number in range(count)]
            new = []
            for w in range(width):
                d = [anchors[w][c] - p[c] for c in range(3)]
                s = d[0] * d[0] + d[1] * d[1] + d[2] * d[2] + p[3]
                root = lax.rsqrt(s)
                inv = root * root
                scale = inv * root * p[16]
                along_b = p[4] * d[0] + p[5] * d[1] + p[6] * d[2]
                along_n = p[7] * d[0] + p[8] * d[1] + p[9] * d[2]
                weight_b = scale * along_n
                weight_n = scale * along_b
                weight_d = scale * (along_b * along_n * inv - p[17])
                for c in range(3):
                    new.append(
                        sums[3 * w + c] + (p[10 + c] * weight_b + p[13 + c] * weight_n + d[c] * weight_d)
                    )
            return tuple(new)

        zero = jnp.zeros((8, LANES), jnp.float32)
        sums = lax.fori_loop(0, loops // 8, loop_step, (zero,) * (3 * width), unroll=2)
        for w in range(width):
            chunk = step * width + w
            for c in range(3):
                total = jnp.sum(sums[3 * w + c], axis=0, keepdims=True)
                part_ref[lax.div(chunk, rows_each), c, pl.ds(lax.rem(chunk, rows_each), 1), :] = (
                    total + (1.0 / nl) * anchor_ref[c, pl.ds(chunk, 1), :]
                )
        return 0

    lax.fori_loop(0, chunks // width, chunk_step, 0)


def split(value):
    high = value.astype(jnp.bfloat16)
    low = (value - high.astype(jnp.float32)).astype(jnp.bfloat16)
    return high, low


def whole_kernel(
    na, nl, atom_total,
    site_ref, cells_ref, burgers_ref, habit_ref, radius_ref, out_ref,
    params_ref, anchor_ref, part_ref, landed_ref, pos_ref, acc_ref,
    left0, right0, left1, right1, own_ref, give_ref, take_ref,
    send_a, recv_a, send_b, recv_b, send_c, recv_c, send_d, recv_d,
):
    me_a = lax.axis_index("atoms")
    me_l = lax.axis_index("loops")
    mesh_ids = pl.DeviceIdType.MESH
    chips = na // 2
    core = lax.rem(me_a, 2)
    peers_a = [lax.rem(me_a + 2 * o, na) for o in range(1, chips)]
    peers_l = [lax.rem(me_l + o, nl) for o in range(1, nl)]
    partner = me_a + 1 - 2 * core
    barrier = pltpu.get_barrier_semaphore()
    for peer in peers_a + [partner]:
        pl.semaphore_signal(barrier, inc=1, device_id=(peer, me_l), device_id_type=mesh_ids)
    for peer in peers_l:
        pl.semaphore_signal(barrier, inc=1, device_id=(me_a, peer), device_id_type=mesh_ids)

    field_phase(
        nl, site_ref, cells_ref, burgers_ref, habit_ref, radius_ref, part_ref, params_ref, anchor_ref
    )
    pl.semaphore_wait(barrier, chips + nl - 1)

    def send(src, dst, send_sem, recv_sem, peer):
        copy = pltpu.make_async_remote_copy(
            src_ref=src,
            dst_ref=dst,
            send_sem=send_sem,
            recv_sem=recv_sem,
            device_id=peer,
            device_id_type=mesh_ids,
        )
        copy.start()
        return copy

    first = [
        send(part_ref.at[peer], landed_ref.at[o], send_a.at[o], recv_a.at[o], (me_a, peer))
        for o, peer in enumerate(peers_l)
    ]

    zrows, xhalf, _ = out_ref.shape
    zhalf, yhalf = zrows // 2, QY // 2
    rows = pos_ref.shape[3]
    half = rows // 2
    inverse = 1.0 / LATTICE
    unit = inverse / QX
    pair = lax.div(me_a, 2)
    xmid = 1.0 + (pair * (2 * xhalf) + xhalf - QX // 2).astype(jnp.float32) / QX
    zmid = (me_l * zrows + zhalf - QZ // 2).astype(jnp.float32) / QX

    def sub_iota(count):
        return lax.broadcasted_iota(jnp.int32, (count, LANES), 0)

    znumber = sub_iota(2 * zhalf)
    zsine = znumber >= zhalf
    zfactor = (jnp.where(zsine, znumber - zhalf, znumber).astype(jnp.float32) + 0.5) * unit
    zshift = jnp.where(zsine, 0.25, 0.0).astype(jnp.float32)
    xfactor = (sub_iota(xhalf).astype(jnp.float32) + 0.5) * unit
    fine = (sub_iota(8).astype(jnp.float32) - 3.5) * unit
    blocks = yhalf // 16
    coarse_number = sub_iota(8)
    coarse = jnp.where(
        coarse_number < blocks, 4.0 + 8.0 * coarse_number.astype(jnp.float32), 0.5 * yhalf
    ) * unit

    def tables(x, y, z):
        ztab = cos_turns(z * zfactor - zshift)
        xtab = cos_sin_turns(x * xfactor)
        base = (x * xmid + z * zmid + y) * inverse
        base = base - jnp.round(base)
        dr, di = cos_sin_turns(base + y * fine)
        cc, cs = cos_sin_turns(y * coarse)
        left = jnp.concatenate(
            [xtab[t][n : n + 1, :] * ztab for t in range(2) for n in range(xhalf)], axis=0
        )
        real = [None] * (2 * blocks)
        imag = [None] * (2 * blocks)
        for k in range(blocks):
            c, s = cc[k : k + 1, :], cs[k : k + 1, :]
            rc, rs, ic, is_ = dr * c, dr * s, di * c, di * s
            real[blocks + k], imag[blocks + k] = rc - is_, ic + rs
            real[blocks - 1 - k], imag[blocks - 1 - k] = rc + is_, ic - rs
        turned = jnp.concatenate(real + imag, axis=0)
        right = jnp.concatenate(
            [turned * cc[blocks : blocks + 1, :], turned * cs[blocks : blocks + 1, :]], axis=0
        )
        return split(left), split(right)

    def build(quarter, slot, begin, left_ref, right_ref):
        for r in range(half):
            x, y, z = (pos_ref[quarter, slot, c, begin + r : begin + r + 1, :] for c in range(3))
            left, right = tables(x, y, z)
            lanes = slice(r * LANES, (r + 1) * LANES)
            for n in range(2):
                left_ref[n, :, lanes] = left[n]
                right_ref[n, :, lanes] = right[n]

    def multiply(left_ref, right_ref):
        lh, ll, rh, rl = left_ref[0], left_ref[1], right_ref[0], right_ref[1]
        acc_ref[...] += lax.dot_general(
            jnp.concatenate([lh, ll, lh], axis=1),
            jnp.concatenate([rh, rh, rl], axis=1),
            (((1,), (1,)), ((), ())),
            preferred_element_type=jnp.float32,
        )

    def process(quarter, begin, end):
        def step(slot, _):
            build(quarter, slot, 0, left0, right0)
            multiply(left1, right1)
            build(quarter, slot, half, left1, right1)
            multiply(left0, right0)
            return 0

        lax.fori_loop(begin, end, step, 0)

    acc_ref[...] = jnp.zeros_like(acc_ref)
    left1[...] = jnp.zeros_like(left1)
    right1[...] = jnp.zeros_like(right1)
    total = part_ref[me_l]
    for o, copy in enumerate(first):
        copy.wait_recv()
        total = total + landed_ref[o]
    pos_ref[0, 0] = total
    second = [
        send(pos_ref.at[0, 0], pos_ref.at[0, o + 1], send_b.at[o], recv_b.at[o], (peer, me_l))
        for o, peer in enumerate(peers_a)
    ]
    process(0, 0, 1)
    for copy in second:
        copy.wait_recv()
    third = [
        send(pos_ref.at[0], pos_ref.at[o + 1], send_c.at[o], recv_c.at[o], (me_a, peer))
        for o, peer in enumerate(peers_l)
    ]
    process(0, 1, chips)
    for o, copy in enumerate(third):
        copy.wait_recv()
        process(o + 1, 0, chips)
    multiply(left1, right1)

    mine = (2 * core - 1).astype(jnp.float32)
    width = 2 * zhalf

    def combine(begin):
        block = acc_ref[begin : begin + width, :]
        cre, cim = block[:, :yhalf], block[:, yhalf : 2 * yhalf]
        sre, sim = block[:, 2 * yhalf : 3 * yhalf], block[:, 3 * yhalf :]
        re = jnp.concatenate([cre + sim, cre - sim], axis=1)
        im = jnp.concatenate([cim - sre, cim + sre], axis=1)
        rc, rs, ic, is_ = re[:zhalf], re[zhalf:], im[:zhalf], im[zhalf:]
        return ((rc + is_, ic - rs), (rc - is_, ic + rs))

    pieces = math.gcd(4, xhalf)
    each = xhalf // pieces
    fourth = []
    for piece in range(pieces):
        for mx in range(piece * each, (piece + 1) * each):
            of_cos = combine(mx * width)
            of_sin = combine((xhalf + mx) * width)
            for zsign in range(2):
                rc, ic = of_cos[zsign]
                rs, is_ = of_sin[zsign][0] * mine, of_sin[zsign][1] * mine
                own_ref[mx, zsign, 0], own_ref[mx, zsign, 1] = rc - is_, ic + rs
                give_ref[mx, zsign, 0], give_ref[mx, zsign, 1] = rc + is_, ic - rs
        at = pl.ds(piece * each, each)
        fourth.append(
            send(give_ref.at[at], take_ref.at[at], send_d.at[piece], recv_d.at[piece], (partner, me_l))
        )
    for piece in range(pieces):
        fourth[piece].wait_recv()
        for mx in range(piece * each, (piece + 1) * each):
            place = core * mx + (1 - core) * (xhalf - 1 - mx)
            for zsign in range(2):
                re = own_ref[mx, zsign, 0] + take_ref[mx, zsign, 0]
                im = own_ref[mx, zsign, 1] + take_ref[mx, zsign, 1]
                value = jnp.log1p((re * re + im * im) / atom_total)
                for mz in range(zhalf):
                    zi = zhalf + mz if zsign else zhalf - 1 - mz
                    out_ref[zi, pl.ds(place, 1), :] = value[mz : mz + 1, :]
    for copy in first + second + third + fourth:
        copy.wait_send()


def body(na, nl, atom_site, loop_cells, loop_burgers, loop_habit, loop_radius):
    atoms = atom_site.shape[0]
    loops = loop_cells.shape[1]
    chunks = atoms // LANES
    rows = chunks // nl
    zrows, xrows = QZ // nl, QX // na
    height = 2 * zrows * xrows
    depth = rows // 2 * LANES
    vmem = pl.BlockSpec(memory_space=pltpu.VMEM)
    f32, bf16 = jnp.float32, jnp.bfloat16
    half_block = (xrows, 2, 2, zrows // 2, QY)
    scratch = [
        pltpu.VMEM((18, loops, LANES), f32),
        pltpu.VMEM((3, chunks, LANES), f32),
        pltpu.VMEM((nl, 3, rows, LANES), f32),
        pltpu.VMEM((nl - 1, 3, rows, LANES), f32),
        pltpu.VMEM((nl, na // 2, 3, rows, LANES), f32),
        pltpu.VMEM((height, 2 * QY), f32),
        pltpu.VMEM((2, height, depth), bf16),
        pltpu.VMEM((2, 2 * QY, depth), bf16),
        pltpu.VMEM((2, height, depth), bf16),
        pltpu.VMEM((2, 2 * QY, depth), bf16),
    ] + [pltpu.VMEM(half_block, f32)] * 3
    counts = (nl - 1, nl - 1, na // 2 - 1, na // 2 - 1, nl - 1, nl - 1, 4, 4)
    scratch += [pltpu.SemaphoreType.DMA((n,)) for n in counts]
    return pl.pallas_call(
        functools.partial(whole_kernel, na, nl, float(atoms * na)),
        out_shape=jax.ShapeDtypeStruct((zrows, xrows, QY), f32),
        in_specs=[vmem] * 5,
        out_specs=vmem,
        scratch_shapes=scratch,
        compiler_params=pltpu.CompilerParams(
            collective_id=0, has_side_effects=True, vmem_limit_bytes=48 * 2**20
        ),
        name="diffuse",
    )(
        atom_site.reshape(chunks, LANES),
        loop_cells,
        loop_burgers.reshape(1, loops),
        loop_habit.reshape(1, loops),
        loop_radius.reshape(1, loops),
    )


def solution(mesh):
    placed = (P("atoms"), P(None, "loops"), P("loops"), P("loops"), P("loops"))
    return jax.shard_map(
        functools.partial(body, mesh.shape["atoms"], mesh.shape["loops"]),
        mesh=mesh,
        in_specs=placed,
        out_specs=P("loops", "atoms", None),
        check_vma=False,
    )
```

time: 57 us -> 45.9 us (0.81)
  Pallas kernels: 55.2 us -> 43.6 us
  local copies, waits for them, and re-layouts: 1.44 us -> 2.1 us
    pallas_call x3 -> x1, Pallas kernels: 55.2 us -> 43.6 us  [body(): pl.pallas_call(functools.partial(whole_kernel, na, nl, float(atoms * na))...]
    unnamed x10 -> x11, local copies, waits for them, and re-layouts: 1.44 us -> 2.1 us
where the time goes in v2:
time: 45.9 us; the launch traced here: 45.7 us
  Pallas kernels  43.6 us (95%)
  local copies, waits for them, and re-layouts  2.1 us (5%)
    pallas_call x1, Pallas kernels, body(): pl.pallas_call(functools.partial(whole_kernel, na, nl, float(atoms * na))...  43.6 us
    unnamed x11, local copies, waits for them, and re-layouts  2.1 us

profile of v2, /device:TPU:0, one launch (start us, length us, event | category | flops | bytes accessed | tf_op | source)
XLA Modules:
  0.0 45.7 jit_solution(549046593466455041)
XLA Ops:
  0.0 0.0 copy-start.1
  0.0 0.0 copy-start.3
  0.0 0.0 copy-start.4
  0.0 0.0 copy-start.2
  0.0 0.7 %copy-done.1 = s32[3,256]{1,0:T(4,128)S(1)} copy-done((s32[3,256]{1,0:T(4,128)S(1)}, s32[3,256]{1,0:T(4,128)}, u32[]{:S(2)}) %copy-start.1) | copy-done | bytes 3096
  0.7 0.0 copy-done.3
  0.7 0.0 copy-done.4
  0.7 0.0 copy-done.2
  0.7 0.0 copy-start
  0.7 0.7 %copy-done = s32[4096]{0:T(1024)S(1)} copy-done((s32[4096]{0:T(1024)S(1)}, s32[4096]{0:T(1024)}, u32[]{:S(2)}) %copy-start) | copy-done | bytes 16408
  1.4 43.6 %diffuse.1 = f32[16,16,128]{2,1,0:T(8,128)S(1)} custom-call(s32[32,128]{1,0:T(8,128)S(1)} %bitcast.4, s32[3,256]{1,0:T(4,128)S(1)} %copy-done.1, s32[1,256]{1,0:T(1,128)S(1)} %bitcast.5, s32[1,256]{1,0:T(1,128)S(1)} %bitcast.6, f32[1,256]{1,0:T(1,128)S(1)} %bitcast.7), custom_call_target="tpu_custom_call" | custom-call | tf_op jit(solution)/shard_map/diffuse/pallas_call | solution.py:375
  45.0 0.7 %copy.7 = f32[16,16,128]{2,1,0:T(8,128)} copy(f32[16,16,128]{2,1,0:T(8,128)S(1)} %diffuse.1) | data formatting | bytes 262144
Async XLA Ops:
  0.0 0.7 %copy-start.1 = (s32[3,256]{1,0:T(4,128)S(1)}, s32[3,256]{1,0:T(4,128)}, u32[]{:S(2)}) copy-start(s32[3,256]{1,0:T(4,128)} %cells_ref.1) | copy-start | bytes 9220
  0.0 0.7 %copy-start.3 = (s32[256]{0:T(256)S(1)}, s32[256]{0:T(256)}, u32[]{:S(2)}) copy-start(s32[256]{0:T(256)} %param.8) | copy-start | bytes 3076
  0.0 0.7 %copy-start.4 = (f32[256]{0:T(256)S(1)}, f32[256]{0:T(256)}, u32[]{:S(2)}) copy-start(f32[256]{0:T(256)} %param.9) | copy-start | bytes 3076
  0.0 0.7 %copy-start.2 = (s32[256]{0:T(256)S(1)}, s32[256]{0:T(256)}, u32[]{:S(2)}) copy-start(s32[256]{0:T(256)} %param.7) | copy-start | bytes 3076
  0.7 0.7 %copy-start = (s32[4096]{0:T(1024)S(1)}, s32[4096]{0:T(1024)}, u32[]{:S(2)}) copy-start(s32[4096]{0:T(1024)} %param.5) | copy-start | bytes 49156

commit v3 on v2

--- a/solution.py
+++ b/solution.py
@@ -15,6 +15,8 @@
 QY = 128
 QZ = 64
 LANES = 128
+SCALE = 128.0
+SMALL = jnp.float8_e4m3fn
 
 LATTICE = 2.8665
 POISSON = 0.29
@@ -156,15 +158,15 @@
 
 def split(value):
     high = value.astype(jnp.bfloat16)
-    low = (value - high.astype(jnp.float32)).astype(jnp.bfloat16)
-    return high, low
+    low = value - high.astype(jnp.float32)
+    return high, value.astype(SMALL), low.astype(SMALL)
 
 
 def whole_kernel(
     na, nl, atom_total,
     site_ref, cells_ref, burgers_ref, habit_ref, radius_ref, out_ref,
     params_ref, anchor_ref, part_ref, landed_ref, pos_ref, acc_ref,
-    left0, right0, left1, right1, own_ref, give_ref, take_ref,
+    tabs0, tabs1, own_ref, give_ref, take_ref,
     send_a, recv_a, send_b, recv_b, send_c, recv_c, send_d, recv_d,
 ):
     me_a = lax.axis_index("atoms")
@@ -229,11 +231,12 @@
     ) * unit
 
     def tables(x, y, z):
-        ztab = cos_turns(z * zfactor - zshift)
+        ztab = SCALE * cos_turns(z * zfactor - zshift)
         xtab = cos_sin_turns(x * xfactor)
         base = (x * xmid + z * zmid + y) * inverse
         base = base - jnp.round(base)
         dr, di = cos_sin_turns(base + y * fine)
+        dr, di = SCALE * dr, SCALE * di
         cc, cs = cos_sin_turns(y * coarse)
         left = jnp.concatenate(
             [xtab[t][n : n + 1, :] * ztab for t in range(2) for n in range(xhalf)], axis=0
@@ -251,37 +254,37 @@
         )
         return split(left), split(right)
 
-    def build(quarter, slot, begin, left_ref, right_ref):
+    def build(quarter, slot, begin, tabs):
         for r in range(half):
             x, y, z = (pos_ref[quarter, slot, c, begin + r : begin + r + 1, :] for c in range(3))
             left, right = tables(x, y, z)
             lanes = slice(r * LANES, (r + 1) * LANES)
-            for n in range(2):
-                left_ref[n, :, lanes] = left[n]
-                right_ref[n, :, lanes] = right[n]
-
-    def multiply(left_ref, right_ref):
-        lh, ll, rh, rl = left_ref[0], left_ref[1], right_ref[0], right_ref[1]
-        acc_ref[...] += lax.dot_general(
-            jnp.concatenate([lh, ll, lh], axis=1),
-            jnp.concatenate([rh, rh, rl], axis=1),
-            (((1,), (1,)), ((), ())),
-            preferred_element_type=jnp.float32,
+            for n, value in enumerate(left + right):
+                tabs[n][:, lanes] = value
+
+    def dot(a, b):
+        return lax.dot_general(
+            a, b, (((1,), (1,)), ((), ())), preferred_element_type=jnp.float32
         )
+
+    def multiply(tabs):
+        lh, lq, ll, rh, rq, rl = (ref[...] for ref in tabs)
+        small = dot(jnp.concatenate([ll, lq], axis=1), jnp.concatenate([rq, rl], axis=1))
+        acc_ref[...] += dot(lh, rh) + small
 
     def process(quarter, begin, end):
         def step(slot, _):
-            build(quarter, slot, 0, left0, right0)
-            multiply(left1, right1)
-            build(quarter, slot, half, left1, right1)
-            multiply(left0, right0)
+            build(quarter, slot, 0, tabs0)
+            multiply(tabs1)
+            build(quarter, slot, half, tabs1)
+            multiply(tabs0)
             return 0
 
         lax.fori_loop(begin, end, step, 0)
 
     acc_ref[...] = jnp.zeros_like(acc_ref)
-    left1[...] = jnp.zeros_like(left1)
-    right1[...] = jnp.zeros_like(right1)
+    for ref in tabs1:
+        ref[...] = jnp.zeros_like(ref)
     total = part_ref[me_l]
     for o, copy in enumerate(first):
         copy.wait_recv()
@@ -302,7 +305,7 @@
     for o, copy in enumerate(third):
         copy.wait_recv()
         process(o + 1, 0, chips)
-    multiply(left1, right1)
+    multiply(tabs1)
 
     mine = (2 * core - 1).astype(jnp.float32)
     width = 2 * zhalf
@@ -365,15 +368,16 @@
         pltpu.VMEM((nl - 1, 3, rows, LANES), f32),
         pltpu.VMEM((nl, na // 2, 3, rows, LANES), f32),
         pltpu.VMEM((height, 2 * QY), f32),
-        pltpu.VMEM((2, height, depth), bf16),
-        pltpu.VMEM((2, 2 * QY, depth), bf16),
-        pltpu.VMEM((2, height, depth), bf16),
-        pltpu.VMEM((2, 2 * QY, depth), bf16),
-    ] + [pltpu.VMEM(half_block, f32)] * 3
+    ]
+    table = tuple(
+        pltpu.VMEM((count, depth), kind) for count in (height, 2 * QY) for kind in (bf16, SMALL, SMALL)
+    )
+    scratch += [table, table]
+    scratch += [pltpu.VMEM(half_block, f32)] * 3
     counts = (nl - 1, nl - 1, na // 2 - 1, na // 2 - 1, nl - 1, nl - 1, 4, 4)
     scratch += [pltpu.SemaphoreType.DMA((n,)) for n in counts]
     return pl.pallas_call(
-        functools.partial(whole_kernel, na, nl, float(atoms * na)),
+        functools.partial(whole_kernel, na, nl, SCALE**4 * atoms * na),
         out_shape=jax.ShapeDtypeStruct((zrows, xrows, QY), f32),
         in_specs=[vmem] * 5,
         out_specs=vmem,

time: 45.9 us -> 43.5 us (0.948)
  Pallas kernels: 43.6 us -> 41.1 us
    pallas_call x1, Pallas kernels: 43.6 us -> 41.1 us  [body(): pl.pallas_call(functools.partial(whole_kernel, na, nl, SCALE ** 4 * atoms...]
where the time goes in v3:
time: 43.5 us; the launch traced here: 43.2 us
  Pallas kernels  41.1 us (94%)
  local copies, waits for them, and re-layouts  2.1 us (5%)
    pallas_call x1, Pallas kernels, body(): pl.pallas_call(functools.partial(whole_kernel, na, nl, SCALE ** 4 * atoms...  41.1 us
    unnamed x11, local copies, waits for them, and re-layouts  2.1 us

profile of v3, /device:TPU:0, one launch (start us, length us, event | category | flops | bytes accessed | tf_op | source)
XLA Modules:
  0.0 43.2 jit_solution(6603440916315103325)
XLA Ops:
  0.0 0.0 copy-start.1
  0.0 0.0 copy-start.3
  0.0 0.0 copy-start.4
  0.0 0.0 copy-start.2
  0.0 0.7 %copy-done.1 = s32[3,256]{1,0:T(4,128)S(1)} copy-done((s32[3,256]{1,0:T(4,128)S(1)}, s32[3,256]{1,0:T(4,128)}, u32[]{:S(2)}) %copy-start.1) | copy-done | bytes 3096
  0.7 0.0 copy-done.3
  0.7 0.0 copy-done.4
  0.7 0.0 copy-done.2
  0.7 0.0 copy-start
  0.7 0.7 %copy-done = s32[4096]{0:T(1024)S(1)} copy-done((s32[4096]{0:T(1024)S(1)}, s32[4096]{0:T(1024)}, u32[]{:S(2)}) %copy-start) | copy-done | bytes 16408
  1.4 41.1 %diffuse.1 = f32[16,16,128]{2,1,0:T(8,128)S(1)} custom-call(s32[32,128]{1,0:T(8,128)S(1)} %bitcast.4, s32[3,256]{1,0:T(4,128)S(1)} %copy-done.1, s32[1,256]{1,0:T(1,128)S(1)} %bitcast.5, s32[1,256]{1,0:T(1,128)S(1)} %bitcast.6, f32[1,256]{1,0:T(1,128)S(1)} %bitcast.7), custom_call_target="tpu_custom_call" | custom-call | tf_op jit(solution)/shard_map/diffuse/pallas_call | solution.py:379
  42.6 0.7 %copy.7 = f32[16,16,128]{2,1,0:T(8,128)} copy(f32[16,16,128]{2,1,0:T(8,128)S(1)} %diffuse.1) | data formatting | bytes 262144
Async XLA Ops:
  0.0 0.7 %copy-start.1 = (s32[3,256]{1,0:T(4,128)S(1)}, s32[3,256]{1,0:T(4,128)}, u32[]{:S(2)}) copy-start(s32[3,256]{1,0:T(4,128)} %cells_ref.1) | copy-start | bytes 9220
  0.0 0.7 %copy-start.3 = (s32[256]{0:T(256)S(1)}, s32[256]{0:T(256)}, u32[]{:S(2)}) copy-start(s32[256]{0:T(256)} %param.8) | copy-start | bytes 3076
  0.0 0.7 %copy-start.4 = (f32[256]{0:T(256)S(1)}, f32[256]{0:T(256)}, u32[]{:S(2)}) copy-start(f32[256]{0:T(256)} %param.9) | copy-start | bytes 3076
  0.0 0.7 %copy-start.2 = (s32[256]{0:T(256)S(1)}, s32[256]{0:T(256)}, u32[]{:S(2)}) copy-start(s32[256]{0:T(256)} %param.7) | copy-start | bytes 3076
  0.7 0.7 %copy-start = (s32[4096]{0:T(1024)S(1)}, s32[4096]{0:T(1024)}, u32[]{:S(2)}) copy-start(s32[4096]{0:T(1024)} %param.5) | copy-start | bytes 49156

commit v4 on v3

--- a/solution.py
+++ b/solution.py
@@ -45,8 +45,8 @@
     return [float(c) for c in series.convert(kind=np.polynomial.Polynomial).coef]
 
 
-COSINE = fit(lambda r: np.cos(2.0 * np.pi * r), 6)
-SINE = fit(lambda r: np.sin(2.0 * np.pi * r) / r, 6)
+COSINE = fit(lambda r: np.cos(2.0 * np.pi * r), 5)
+SINE = fit(lambda r: np.sin(2.0 * np.pi * r) / r, 5)
 
 
 def horner(coefs, u):
@@ -231,7 +231,11 @@
     ) * unit
 
     def tables(x, y, z):
-        ztab = SCALE * cos_turns(z * zfactor - zshift)
+        if zhalf % 8 == 0:
+            ztab = jnp.concatenate(cos_sin_turns(z * zfactor[:zhalf]), axis=0)
+        else:
+            ztab = cos_turns(z * zfactor - zshift)
+        ztab = SCALE * ztab
         xtab = cos_sin_turns(x * xfactor)
         base = (x * xmid + z * zmid + y) * inverse
         base = base - jnp.round(base)
@@ -254,8 +258,8 @@
         )
         return split(left), split(right)
 
-    def build(quarter, slot, begin, tabs):
-        for r in range(half):
+    def build(quarter, slot, begin, span, tabs):
+        for r in range(*span):
             x, y, z = (pos_ref[quarter, slot, c, begin + r : begin + r + 1, :] for c in range(3))
             left, right = tables(x, y, z)
             lanes = slice(r * LANES, (r + 1) * LANES)
@@ -267,17 +271,22 @@
             a, b, (((1,), (1,)), ((), ())), preferred_element_type=jnp.float32
         )
 
-    def multiply(tabs):
-        lh, lq, ll, rh, rq, rl = (ref[...] for ref in tabs)
-        small = dot(jnp.concatenate([ll, lq], axis=1), jnp.concatenate([rq, rl], axis=1))
-        acc_ref[...] += dot(lh, rh) + small
+    def multiply_high(tabs):
+        acc_ref[...] += dot(tabs[0][...], tabs[3][...])
+
+    def multiply_rest(tabs):
+        lq, ll, rq, rl = (tabs[n][...] for n in (1, 2, 4, 5))
+        acc_ref[...] += dot(jnp.concatenate([ll, lq], axis=1), jnp.concatenate([rq, rl], axis=1))
+
+    middle = half // 2
 
     def process(quarter, begin, end):
         def step(slot, _):
-            build(quarter, slot, 0, tabs0)
-            multiply(tabs1)
-            build(quarter, slot, half, tabs1)
-            multiply(tabs0)
+            for begin, tabs, ready in ((0, tabs0, tabs1), (half, tabs1, tabs0)):
+                multiply_high(ready)
+                build(quarter, slot, begin, (0, middle), tabs)
+                multiply_rest(ready)
+                build(quarter, slot, begin, (middle, half), tabs)
             return 0
 
         lax.fori_loop(begin, end, step, 0)
@@ -305,7 +314,8 @@
     for o, copy in enumerate(third):
         copy.wait_recv()
         process(o + 1, 0, chips)
-    multiply(tabs1)
+    multiply_high(tabs1)
+    multiply_rest(tabs1)
 
     mine = (2 * core - 1).astype(jnp.float32)
     width = 2 * zhalf

time: 43.5 us -> 43.5 us (level)
  no operation moved by 1% of the time
where the time goes in v4:
time: 43.5 us; the launch traced here: 43.3 us
  Pallas kernels  41.1 us (94%)
  local copies, waits for them, and re-layouts  2.1 us (5%)
    pallas_call x1, Pallas kernels, body(): pl.pallas_call(functools.partial(whole_kernel, na, nl, SCALE ** 4 * atoms...  41.1 us
    unnamed x11, local copies, waits for them, and re-layouts  2.1 us

profile of v4, /device:TPU:0, one launch (start us, length us, event | category | flops | bytes accessed | tf_op | source)
XLA Modules:
  0.0 43.3 jit_solution(14546850479449782010)
XLA Ops:
  0.0 0.0 copy-start.1
  0.0 0.0 copy-start.3
  0.0 0.0 copy-start.4
  0.0 0.0 copy-start.2
  0.0 0.7 %copy-done.1 = s32[3,256]{1,0:T(4,128)S(1)} copy-done((s32[3,256]{1,0:T(4,128)S(1)}, s32[3,256]{1,0:T(4,128)}, u32[]{:S(2)}) %copy-start.1) | copy-done | bytes 3096
  0.7 0.0 copy-done.3
  0.7 0.0 copy-done.4
  0.7 0.0 copy-done.2
  0.7 0.0 copy-start
  0.7 0.7 %copy-done = s32[4096]{0:T(1024)S(1)} copy-done((s32[4096]{0:T(1024)S(1)}, s32[4096]{0:T(1024)}, u32[]{:S(2)}) %copy-start) | copy-done | bytes 16408
  1.4 41.1 %diffuse.1 = f32[16,16,128]{2,1,0:T(8,128)S(1)} custom-call(s32[32,128]{1,0:T(8,128)S(1)} %bitcast.4, s32[3,256]{1,0:T(4,128)S(1)} %copy-done.1, s32[1,256]{1,0:T(1,128)S(1)} %bitcast.5, s32[1,256]{1,0:T(1,128)S(1)} %bitcast.6, f32[1,256]{1,0:T(1,128)S(1)} %bitcast.7), custom_call_target="tpu_custom_call" | custom-call | tf_op jit(solution)/shard_map/diffuse/pallas_call | solution.py:389
  42.6 0.7 %copy.7 = f32[16,16,128]{2,1,0:T(8,128)} copy(f32[16,16,128]{2,1,0:T(8,128)S(1)} %diffuse.1) | data formatting | bytes 262144
Async XLA Ops:
  0.0 0.7 %copy-start.1 = (s32[3,256]{1,0:T(4,128)S(1)}, s32[3,256]{1,0:T(4,128)}, u32[]{:S(2)}) copy-start(s32[3,256]{1,0:T(4,128)} %cells_ref.1) | copy-start | bytes 9220
  0.0 0.7 %copy-start.3 = (s32[256]{0:T(256)S(1)}, s32[256]{0:T(256)}, u32[]{:S(2)}) copy-start(s32[256]{0:T(256)} %param.8) | copy-start | bytes 3076
  0.0 0.7 %copy-start.4 = (f32[256]{0:T(256)S(1)}, f32[256]{0:T(256)}, u32[]{:S(2)}) copy-start(f32[256]{0:T(256)} %param.9) | copy-start | bytes 3076
  0.0 0.7 %copy-start.2 = (s32[256]{0:T(256)S(1)}, s32[256]{0:T(256)}, u32[]{:S(2)}) copy-start(s32[256]{0:T(256)} %param.7) | copy-start | bytes 3076
  0.7 0.7 %copy-start = (s32[4096]{0:T(1024)S(1)}, s32[4096]{0:T(1024)}, u32[]{:S(2)}) copy-start(s32[4096]{0:T(1024)} %param.5) | copy-start | bytes 49156

commit v5 on v4

--- a/solution.py
+++ b/solution.py
@@ -143,7 +143,7 @@
             return tuple(new)
 
         zero = jnp.zeros((8, LANES), jnp.float32)
-        sums = lax.fori_loop(0, loops // 8, loop_step, (zero,) * (3 * width), unroll=2)
+        sums = lax.fori_loop(0, loops // 8, loop_step, (zero,) * (3 * width), unroll=4)
         for w in range(width):
             chunk = step * width + w
             for c in range(3):
@@ -164,11 +164,26 @@
 
 def whole_kernel(
     na, nl, atom_total,
-    site_ref, cells_ref, burgers_ref, habit_ref, radius_ref, out_ref,
+    site_any, cells_any, burgers_any, habit_any, radius_any, out_ref,
+    site_ref, cells_ref, burgers_ref, habit_ref, radius_ref, fetched,
     params_ref, anchor_ref, part_ref, landed_ref, pos_ref, acc_ref,
     tabs0, tabs1, own_ref, give_ref, take_ref,
     send_a, recv_a, send_b, recv_b, send_c, recv_c, send_d, recv_d,
 ):
+    fetches = [
+        pltpu.make_async_copy(source, held, fetched.at[n])
+        for n, (source, held) in enumerate(
+            (
+                (site_any, site_ref),
+                (cells_any, cells_ref),
+                (burgers_any, burgers_ref),
+                (habit_any, habit_ref),
+                (radius_any, radius_ref),
+            )
+        )
+    ]
+    for copy in fetches:
+        copy.start()
     me_a = lax.axis_index("atoms")
     me_l = lax.axis_index("loops")
     mesh_ids = pl.DeviceIdType.MESH
@@ -183,6 +198,8 @@
     for peer in peers_l:
         pl.semaphore_signal(barrier, inc=1, device_id=(me_a, peer), device_id_type=mesh_ids)
 
+    for copy in fetches:
+        copy.wait()
     field_phase(
         nl, site_ref, cells_ref, burgers_ref, habit_ref, radius_ref, part_ref, params_ref, anchor_ref
     )
@@ -372,6 +389,12 @@
     f32, bf16 = jnp.float32, jnp.bfloat16
     half_block = (xrows, 2, 2, zrows // 2, QY)
     scratch = [
+        pltpu.VMEM((chunks, LANES), jnp.int32),
+        pltpu.VMEM((3, loops), jnp.int32),
+        pltpu.VMEM((1, loops), jnp.int32),
+        pltpu.VMEM((1, loops), jnp.int32),
+        pltpu.VMEM((1, loops), f32),
+        pltpu.SemaphoreType.DMA((5,)),
         pltpu.VMEM((18, loops, LANES), f32),
         pltpu.VMEM((3, chunks, LANES), f32),
         pltpu.VMEM((nl, 3, rows, LANES), f32),
@@ -389,7 +412,7 @@
     return pl.pallas_call(
         functools.partial(whole_kernel, na, nl, SCALE**4 * atoms * na),
         out_shape=jax.ShapeDtypeStruct((zrows, xrows, QY), f32),
-        in_specs=[vmem] * 5,
+        in_specs=[pl.BlockSpec(memory_space=pl.ANY)] * 5,
         out_specs=vmem,
         scratch_shapes=scratch,
         compiler_params=pltpu.CompilerParams(

time: 43.5 us -> 43.8 us (level)
  no operation moved by 1% of the time
where the time goes in v5:
time: 43.8 us; the launch traced here: 43.5 us
  Pallas kernels  41.4 us (95%)
  local copies, waits for them, and re-layouts  2.1 us (5%)
    pallas_call x1, Pallas kernels, body(): pl.pallas_call(functools.partial(whole_kernel, na, nl, SCALE ** 4 * atoms...  41.4 us
    unnamed x11, local copies, waits for them, and re-layouts  2.1 us

profile of v5, /device:TPU:0, one launch (start us, length us, event | category | flops | bytes accessed | tf_op | source)
XLA Modules:
  0.0 43.5 jit_solution(6912403583334189920)
XLA Ops:
  0.0 0.0 copy-start.1
  0.0 0.0 copy-start.3
  0.0 0.0 copy-start.4
  0.0 0.0 copy-start.2
  0.0 0.7 %copy-done.1 = s32[3,256]{1,0:T(4,128)S(1)} copy-done((s32[3,256]{1,0:T(4,128)S(1)}, s32[3,256]{1,0:T(4,128)}, u32[]{:S(2)}) %copy-start.1) | copy-done | bytes 3096
  0.7 0.0 copy-done.3
  0.7 0.0 copy-done.4
  0.7 0.0 copy-done.2
  0.7 0.0 copy-start
  0.7 0.7 %copy-done = s32[4096]{0:T(1024)S(1)} copy-done((s32[4096]{0:T(1024)S(1)}, s32[4096]{0:T(1024)}, u32[]{:S(2)}) %copy-start) | copy-done | bytes 16408
  1.4 41.4 %diffuse.1 = f32[16,16,128]{2,1,0:T(8,128)S(1)} custom-call(s32[32,128]{1,0:T(8,128)S(1)} %bitcast.4, s32[3,256]{1,0:T(4,128)S(1)} %copy-done.1, s32[1,256]{1,0:T(1,128)S(1)} %bitcast.5, s32[1,256]{1,0:T(1,128)S(1)} %bitcast.6, f32[1,256]{1,0:T(1,128)S(1)} %bitcast.7), custom_call_target="tpu_custom_call" | custom-call | tf_op jit(solution)/shard_map/diffuse/pallas_call | solution.py:412
  42.9 0.7 %copy.7 = f32[16,16,128]{2,1,0:T(8,128)} copy(f32[16,16,128]{2,1,0:T(8,128)S(1)} %diffuse.1) | data formatting | bytes 262144
Async XLA Ops:
  0.0 0.7 %copy-start.1 = (s32[3,256]{1,0:T(4,128)S(1)}, s32[3,256]{1,0:T(4,128)}, u32[]{:S(2)}) copy-start(s32[3,256]{1,0:T(4,128)} %cells_any.1) | copy-start | bytes 9220
  0.0 0.7 %copy-start.3 = (s32[256]{0:T(256)S(1)}, s32[256]{0:T(256)}, u32[]{:S(2)}) copy-start(s32[256]{0:T(256)} %param.8) | copy-start | bytes 3076
  0.0 0.7 %copy-start.4 = (f32[256]{0:T(256)S(1)}, f32[256]{0:T(256)}, u32[]{:S(2)}) copy-start(f32[256]{0:T(256)} %param.9) | copy-start | bytes 3076
  0.0 0.7 %copy-start.2 = (s32[256]{0:T(256)S(1)}, s32[256]{0:T(256)}, u32[]{:S(2)}) copy-start(s32[256]{0:T(256)} %param.7) | copy-start | bytes 3076
  0.7 0.7 %copy-start = (s32[4096]{0:T(1024)S(1)}, s32[4096]{0:T(1024)}, u32[]{:S(2)}) copy-start(s32[4096]{0:T(1024)} %param.5) | copy-start | bytes 49156
